TPU v7x, 32 devices: a whole 2x2x4 slice. The times are simulated.
32 devices in a mesh: groups: 2 (over y), loop: 4 (over z), enc: 2 (over x), rep: 2 (over core).
Axes of the slice: x: 2, y: 2, z: 4, core: 2. Of those that a mesh axis runs over, the one named last changes fastest.
Arguments:
- embeddings: bfloat16 [4096, 768], P(('groups', 'loop', 'rep'), 'enc'), parts along dimension 0, may hold values from -24 to 24
- head_weight: bfloat16 [768, 768], P('enc'), may hold values from -0.21875 to 0.21875
- gp_weights: float32 [4096], P('groups'), parts along dimension 0, may hold values from -24 to 24
- counts: int32 [8], P('groups'), parts along dimension 0, may hold values from 64 to 512, as said below
Outputs:
- embed_grad: bfloat16 [4096, 768], P(('groups', 'loop', 'rep'), 'enc'), parts along dimension 0
- head_grad: float32 [1536, 768], P(('groups', 'enc')), parts along dimension 0
There are 2 independent parts, one for each index of `groups`. A program takes and returns all parts, laid end to end along the dimension named above; an argument that names none is the same for every part. Nothing has to cross between parts.
Inputs may be any that keep to these rules, and one draw needn't show every extreme that they name: `counts`: some block is full and some block holds exactly 64 valid molecules.
All inputs are finite; a program needn't handle non-finite values.
Results may differ from a plain program's by a relative error of at most 0.019.
Values may be sent and summed in bfloat16 or wider, within the bound.
A program may use at most 64 MiB of HBM per device.

v0:
```python
import jax
import jax.numpy as jnp
from jax import lax
from jax.sharding import PartitionSpec as P

EPSILON = 1e-06


def passed_along(value, axis, steps):
    count = lax.axis_size(axis)
    pairs = [(source, (source + steps) % count) for source in range(count)]
    return lax.ppermute(value, axis, pairs)


def pass_forward(piece):
    return passed_along(piece, "loop", 1)


def body(embeddings, head_weight, gp_weights, counts):
    enc_size = lax.axis_size("enc")
    rep_size = lax.axis_size("rep")
    loop_size = lax.axis_size("loop")
    share_rows = embeddings.shape[0]
    piece_rows = share_rows // enc_size
    block_rows = share_rows * rep_size
    loop_index = lax.axis_index("loop")
    enc_index = lax.axis_index("enc")
    rep_index = lax.axis_index("rep")
    rows = embeddings
    own_feats = lax.psum_scatter(
        jnp.dot(rows, head_weight, preferred_element_type=jnp.float32),
        "enc",
        scatter_dimension=0,
        tiled=True,
    ).astype(jnp.bfloat16)
    block_feats = lax.all_gather(own_feats, ("enc", "rep"), axis=0, tiled=True)
    block_norms = jnp.sum(jnp.square(block_feats.astype(jnp.float32)), axis=1)
    offsets = (
        jnp.arange(rep_size, dtype=jnp.int32)[None, :, None] * share_rows
        + jnp.arange(enc_size, dtype=jnp.int32)[:, None, None] * piece_rows
        + jnp.arange(piece_rows, dtype=jnp.int32)[None, None, :]
    ).reshape(block_rows)
    own_base = lax.dynamic_slice_in_dim(gp_weights, loop_index * block_rows, block_rows)
    block_coef = (
        own_base.reshape(rep_size, enc_size, piece_rows).transpose(1, 0, 2).reshape(block_rows)
    )
    own_count = lax.dynamic_index_in_dim(counts, loop_index, keepdims=False)
    block_coef = jnp.where(offsets < own_count, block_coef, 0.0)
    piece_start = rep_index * share_rows + enc_index * piece_rows
    piece_offsets = piece_start + jnp.arange(piece_rows, dtype=jnp.int32)

    def tile(state, piece, anchor):
        anchor_count = lax.dynamic_index_in_dim(counts, anchor, keepdims=False)
        accum, quotient_sum = state
        piece_coef = lax.dynamic_slice_in_dim(
            gp_weights, anchor * block_rows + piece_start, piece_rows
        )
        piece_coef = jnp.where(piece_offsets < anchor_count, piece_coef, 0.0)
        piece_norms = jnp.sum(jnp.square(piece.astype(jnp.float32)), axis=1)
        scores = lax.dot_general(
            piece, block_feats, (((1,), (1,)), ((), ())), preferred_element_type=jnp.float32
        )
        denom = piece_norms[:, None] + block_norms[None, :] - scores + EPSILON
        inverse = 1.0 / (denom * denom)
        pair_coef = piece_coef[:, None] * block_coef[None, :]
        pair_weight = (pair_coef * (piece_norms[:, None] + block_norms[None, :]) * inverse).astype(
            jnp.bfloat16
        )
        quotient_sum = quotient_sum + jnp.sum(pair_coef * 2.0 * scores * inverse, axis=0)
        accum = accum + lax.dot_general(
            pair_weight, piece, (((0,), (0,)), ((), ())), preferred_element_type=jnp.float32
        )
        return (accum, quotient_sum)

    start_state = (
        jnp.zeros((block_rows, block_feats.shape[1]), jnp.float32),
        jnp.zeros((block_rows,), jnp.float32),
    )
    state = tile(start_state, own_feats, loop_index)

    def forward_step(step_index, carry):
        moving, inner = carry
        moving = pass_forward(moving)
        inner = tile(inner, moving, (loop_index - step_index - 1 + loop_size) % loop_size)
        return (moving, inner)

    moving, state = lax.fori_loop(0, loop_size - 1, forward_step, (own_feats, state))
    accum, quotient_sum = state
    grad_block = accum - block_feats.astype(jnp.float32) * quotient_sum[:, None]
    own_grad = lax.psum_scatter(
        grad_block.astype(jnp.bfloat16), ("enc", "rep"), scatter_dimension=0, tiled=True
    )
    piece = lax.all_gather(own_grad, "enc", axis=0, tiled=True)
    back = lax.dot_general(
        piece, head_weight, (((1,), (1,)), ((), ())), preferred_element_type=jnp.float32
    )
    embed_part = back
    rows = embeddings
    head_part = lax.dot_general(
        rows, piece, (((0,), (0,)), ((), ())), preferred_element_type=jnp.float32
    )
    embed_part, head_part = (embed_part, head_part)
    head_grad = lax.psum(head_part, ("loop", "rep"))
    return (embed_part.astype(jnp.bfloat16), head_grad)


def solution(mesh):
    placed = (P(("groups", "loop", "rep"), "enc"), P("enc", None), P("groups"), P("groups"))
    return jax.shard_map(
        body,
        mesh=mesh,
        in_specs=placed,
        out_specs=(P(("groups", "loop", "rep"), "enc"), P(("groups", "enc"), None)),
        check_vma=False,
    )
```

profile of v0, /device:TPU:0, one launch (start us, length us, event | category | flops | bytes accessed | tf_op | source)
XLA Modules:
  0.0 170.0 jit_solution(11172648524668776611)
XLA Ops:
  7.2 1.0 copy-done
  8.2 2.2 %fusion.40 = f32[256,768]{1,0:T(8,128)} fusion(bf16[256,384]{1,0:T(8,128)(2,1)} %param.6, bf16[384,768]{1,0:T(8,128)(2,1)S(1)} %copy-done), kind=kOutput, calls=%fused_computation.56 | convolution fusion | flops 150994944 | bytes 1572864 | tf_op jit(solution)/shard_map/dot_general | solution.py:31
  10.5 0.7 dynamic_slice.37
  11.2 0.8 dynamic_slice.39
  12.0 0.8 compare_select_fusion.1
  12.8 1.5 compare_select_fusion.2
  14.2 16.8 %reduce-scatter.3.cloned.1.call-done = f32[128,768]{1,0:T(8,128)} async-done(((f32[256,768]{1,0:T(8,128)}), f32[128,768]{1,0:T(8,128)}) %reduce-scatter.3.cloned.1.call-update) | async-done | bytes 393232 | tf_op jit(solution)/shard_map/reduce_scatter | solution.py:30
  31.0 1.1 multiply_reduce_fusion.1
  32.1 8.2 %all_gather.6 = bf16[512,768]{1,0:T(8,128)(2,1)S(1)} all-gather(bf16[128,768]{1,0:T(8,128)(2,1)S(1)} %get-tuple-element.541), channel_id=1, replica_groups=mesh['groups'=2,'loop'=4,'enc'=2,'rep'=2] {'enc','rep'}, dimensions={0}, use_global_device_ids=true | all-gather | bytes 983040 | tf_op jit(solution)/shard_map/all_gather | solution.py:36
  41.0 0.5 fusion.30
  41.5 28.3 %while.23 = (s32[]{:T(128)}, bf16[128,768]{1,0:T(8,128)(2,1)S(1)}, f32[512,768]{1,0:T(8,128)S(1)}, f32[512]{0:T(512)S(1)}, s32[]{:T(128)}, /*index=5*/s32[4]{0:T...) while((s32[]{:T(128)}, bf16[128,768]{1,0:T(8,128)(2,1)S(1)}, ...), condition=%wide.region_7.8_spmd.clone.clone, body=%wide.region_4.7_spmd.clone.clone.sunk | while | flops 203260192 | bytes 6246334 | solution.py:87
  41.5 1.5 collective-permute-start
  43.1 0.6 dynamic_slice.49
  43.6 1.4 compare_select_fusion.4
  45.1 5.5 %collective-permute-done = bf16[128,768]{1,0:T(8,128)(2,1)S(1)} collective-permute-done((bf16[128,768]{1,0:T(8,128)(2,1)S(1)}, bf16[128,768]{1,0:T(8,128)(2,1)S(1)}, u32[]{:S(2)}, u32[]{:S(2)}) %collective-permute-start) | collective-permute-done | bytes 196640 | tf_op jit(solution)/shard_map/while/body/eval_jaxpr/ppermute | solution.py:12
  50.6 0.4 fusion.62
  51.1 0.6 convolution_add_fusion.2
  51.8 0.6 dynamic_slice.49
  52.4 1.4 compare_select_fusion.4
  53.8 6.1 %collective-permute-done = bf16[128,768]{1,0:T(8,128)(2,1)S(1)} collective-permute-done((bf16[128,768]{1,0:T(8,128)(2,1)S(1)}, bf16[128,768]{1,0:T(8,128)(2,1)S(1)}, u32[]{:S(2)}, u32[]{:S(2)}) %collective-permute-start) | collective-permute-done | bytes 196640 | tf_op jit(solution)/shard_map/while/body/eval_jaxpr/ppermute | solution.py:12
  60.5 0.6 convolution_add_fusion.2
  61.2 0.6 dynamic_slice.49
  61.8 1.4 compare_select_fusion.4
  63.2 5.4 %collective-permute-done = bf16[128,768]{1,0:T(8,128)(2,1)S(1)} collective-permute-done((bf16[128,768]{1,0:T(8,128)(2,1)S(1)}, bf16[128,768]{1,0:T(8,128)(2,1)S(1)}, u32[]{:S(2)}, u32[]{:S(2)}) %collective-permute-start) | collective-permute-done | bytes 196640 | tf_op jit(solution)/shard_map/while/body/eval_jaxpr/ppermute | solution.py:12
  69.2 0.6 convolution_add_fusion.2
  69.8 1.1 fusion.21
  71.1 20.9 %reduce-scatter.5.cloned.1.call-done = bf16[128,768]{1,0:T(8,128)(2,1)} async-done(((bf16[512,768]{1,0:T(8,128)(2,1)}), bf16[128,768]{1,0:T(8,128)(2,1)}) %reduce-scatter.5.cloned.1.call-update) | async-done | bytes 196624 | tf_op jit(solution)/shard_map/reduce_scatter | solution.py:90
  92.0 7.5 %all_gather.7 = bf16[256,768]{1,0:T(8,128)(2,1)S(1)} all-gather(bf16[128,768]{1,0:T(8,128)(2,1)} %reduce-scatter.5.cloned.1.call-done), channel_id=1, replica_groups=mesh['groups'=2,'loop'=4,'enc'=2,'rep'=2] {'enc'}, dimensions={0}, use_global_device_ids=true | all-gather | bytes 589824 | tf_op jit(solution)/shard_map/all_gather | solution.py:93
  99.5 1.4 convolution_bitcast_fusion
  100.9 1.1 convolution_convert_fusion
  102.0 58.8 %all-reduce.2.cloned.1.call-done = f32[384,768]{0,1:T(8,128)} async-done(((f32[384,768]{0,1:T(8,128)}), f32[384,768]{0,1:T(8,128)}) %all-reduce.2.cloned.1.call-update) | async-done | bytes 1179664 | tf_op jit(solution)/shard_map/psum | solution.py:103
  160.8 2.7 %copy.9 = f32[384,768]{1,0:T(8,128)} copy(f32[384,768]{0,1:T(8,128)} %all-reduce.2.cloned.1.call-done) | data formatting | bytes 2359296
  (29 shorter events, 2.4 us)
Async XLA Ops:
  7.2 1.1 copy-start
  7.2 3.3 %copy-start.2 = (s32[4]{0:T(128)S(1)}, s32[4]{0:T(128)}, u32[]{:S(2)}) copy-start(s32[4]{0:T(128)} %param.9) | copy-start | bytes 52
  7.2 23.8 %reduce-scatter.3.cloned.1.call-start = ((), (), s32[]{:S(2)}) async-start(), calls=%async_computation.2 | async-start | bytes 1179648 | tf_op jit(solution)/shard_map/reduce_scatter | solution.py:30
  10.4 81.6 %reduce-scatter.5.cloned.1.call-start = ((), (), s32[]{:S(2)}) async-start(), calls=%async_computation.3 | async-start | bytes 983040 | tf_op jit(solution)/shard_map/reduce_scatter | solution.py:90
  41.5 9.0 %collective-permute-start = (bf16[128,768]{1,0:T(8,128)(2,1)S(1)}, bf16[128,768]{1,0:T(8,128)(2,1)S(1)}, u32[]{:S(2)}, u32[]{:S(2)}) collective-permute-start(bf16[128,768]{1,0:T(8,128)(2,1)S(1)} %get-tuple-element.558), channel_id=1, source_target_pairs={{0,4},{4,8},{8,12},{12,0},{1,5},{5,9},{9,13},{13,1},{2,6},{6,10},{... | collective-permute-start | bytes 589832 | tf_op jit(solution)/shard_map/while/body/eval_jaxpr/ppermute | solution.py:12
  51.7 8.2 %collective-permute-start = (bf16[128,768]{1,0:T(8,128)(2,1)S(1)}, bf16[128,768]{1,0:T(8,128)(2,1)S(1)}, u32[]{:S(2)}, u32[]{:S(2)}) collective-permute-start(bf16[128,768]{1,0:T(8,128)(2,1)S(1)} %get-tuple-element.558), channel_id=1, source_target_pairs={{0,4},{4,8},{8,12},{12,0},{1,5},{5,9},{9,13},{13,1},{2,6},{6,10},{... | collective-permute-start | bytes 589832 | tf_op jit(solution)/shard_map/while/body/eval_jaxpr/ppermute | solution.py:12
  61.1 7.5 %collective-permute-start = (bf16[128,768]{1,0:T(8,128)(2,1)S(1)}, bf16[128,768]{1,0:T(8,128)(2,1)S(1)}, u32[]{:S(2)}, u32[]{:S(2)}) collective-permute-start(bf16[128,768]{1,0:T(8,128)(2,1)S(1)} %get-tuple-element.558), channel_id=1, source_target_pairs={{0,4},{4,8},{8,12},{12,0},{1,5},{5,9},{9,13},{13,1},{2,6},{6,10},{... | collective-permute-start | bytes 589832 | tf_op jit(solution)/shard_map/while/body/eval_jaxpr/ppermute | solution.py:12
  69.8 29.7 %copy-start.1 = (bf16[256,384]{1,0:T(8,128)(2,1)S(1)}, bf16[256,384]{1,0:T(8,128)(2,1)}, u32[]{:S(2)}) copy-start(bf16[256,384]{1,0:T(8,128)(2,1)} %param.6) | copy-start | bytes 589828
  71.0 89.8 %all-reduce.2.cloned.1.call-start = ((), (), s32[]{:S(2)}) async-start(), calls=%async_computation.4 | async-start | bytes 2359296 | tf_op jit(solution)/shard_map/psum | solution.py:103
Sparse Core Ops, SparseCore 0:
  10.8 20.1 reduce-scatter.2
  71.1 20.8 reduce-scatter.4
  101.1 59.6 all-reduce.1
where the time goes:
time: 170 us
  waiting for transfers between devices  114 us (67%)
  blocking collectives  15.7 us (9%)
  between operations  13.8 us (8%)
  other arithmetic  9.37 us (6%)
  matrix products  8.66 us (5%)
  local copies, waits for them, and re-layouts  6.9 us (4%)
  starting transfers between devices  1.78 us (1%)
    psum x1, waiting for transfers between devices, body(): head_grad = lax.psum(head_part, ('loop', 'rep'))  58.8 us
    reduce_scatter x1, waiting for transfers between devices, body(): lax.psum_scatter(grad_block.astype(jnp.bfloat16), ('enc', 'rep'), scatter...  20.9 us
    ppermute x3, waiting for transfers between devices, passed_along(): return lax.ppermute(value, axis, pairs)  17 us
    reduce_scatter x1, waiting for transfers between devices, body(): lax.psum_scatter(jnp.dot(rows, head_weight, preferred_element_type=jnp.fl...  16.8 us
    all_gather x1, blocking collectives, body(): block_feats = lax.all_gather(own_feats, ('enc', 'rep'), axis=0, tiled=True)  8.2 us
    all_gather x1, blocking collectives, body(): piece = lax.all_gather(own_grad, 'enc', axis=0, tiled=True)  7.51 us
    select_n x4, other arithmetic, tile(): piece_coef = jnp.where(piece_offsets < anchor_count, piece_coef, 0.0)  5.68 us
    unnamed x7, local copies, waits for them, and re-layouts  3.67 us
  transfers between devices with their start and end apart: 6, of which 6 were waited for; matrix products, arithmetic and copies ran while one was open for 6% of the time, Pallas kernels for 0%

commit v1 on v0

--- a/solution.py
+++ b/solution.py
@@ -33,7 +33,18 @@
         scatter_dimension=0,
         tiled=True,
     ).astype(jnp.bfloat16)
-    block_feats = lax.all_gather(own_feats, ("enc", "rep"), axis=0, tiled=True)
+    ways = lax.axis_size(("enc", "rep"))
+    up = [(d, (d + 1) % ways) for d in range(ways)]
+    down = [(d, (d - 1) % ways) for d in range(ways)]
+    earlier, later = ([own_feats], [own_feats])
+    for _ in range(ways // 2):
+        earlier.append(lax.ppermute(earlier[-1], ("enc", "rep"), up))
+    for _ in range((ways - 1) // 2):
+        later.append(lax.ppermute(later[-1], ("enc", "rep"), down))
+    line = jnp.concatenate([*earlier[::-1], *later[1:]], axis=0)
+    block_feats = jnp.roll(
+        line, (lax.axis_index(("enc", "rep")) - ways // 2) * own_feats.shape[0], axis=0
+    )
     block_norms = jnp.sum(jnp.square(block_feats.astype(jnp.float32)), axis=1)
     offsets = (
         jnp.arange(rep_size, dtype=jnp.int32)[None, :, None] * share_rows

time: 170 us -> 176 us (1.035)
  waiting for transfers between devices: 114 us -> 125 us
  blocking collectives: 15.7 us -> 7.53 us
  starting transfers between devices: 1.78 us -> 3.57 us
    all_gather x1 -> x0, blocking collectives: 8.2 us -> none  [body(): block_feats = lax.all_gather(own_feats, ('enc', 'rep'), axis=0, tiled=True)]
    ppermute x0 -> x3, waiting for transfers between devices: none -> 8.13 us  [the longest x2 6.27 us: body(): earlier.append(lax.ppermute(earlier[-1], ('enc', 'rep'), up))]
    reduce_scatter x1, waiting for transfers between devices: 16.8 us -> 19.2 us  [body(): lax.psum_scatter(jnp.dot(rows, head_weight, preferred_element_type=jnp.fl...]
    ppermute x0 -> x3, starting transfers between devices: none -> 1.8 us  [the longest x1 1.74 us: body(): later.append(lax.ppermute(later[-1], ('enc', 'rep'), down))]
    unnamed x7 -> x14, local copies, waits for them, and re-layouts: 3.67 us -> 3.77 us
  transfers between devices with their start and end apart: 6 -> 9, of which waited for: 6 -> 9; matrix products, arithmetic and copies ran while one was open for 6% -> 6% of each run, Pallas kernels for 0% -> 0%
where the time goes in v1:
time: 176 us; the launch traced here: 175 us
  waiting for transfers between devices  125 us (71%)
  between operations  13.9 us (8%)
  other arithmetic  9.38 us (5%)
  matrix products  8.66 us (5%)
  blocking collectives  7.53 us (4%)
  local copies, waits for them, and re-layouts  7.19 us (4%)
  starting transfers between devices  3.57 us (2%)
    psum x1, waiting for transfers between devices, body(): head_grad = lax.psum(head_part, ('loop', 'rep'))  58.7 us
    reduce_scatter x1, waiting for transfers between devices, body(): lax.psum_scatter(grad_block.astype(jnp.bfloat16), ('enc', 'rep'), scatter...  21.7 us
    reduce_scatter x1, waiting for transfers between devices, body(): lax.psum_scatter(jnp.dot(rows, head_weight, preferred_element_type=jnp.fl...  19.2 us
    ppermute x3, waiting for transfers between devices, passed_along(): return lax.ppermute(value, axis, pairs)  17.3 us
    all_gather x1, blocking collectives, body(): piece = lax.all_gather(own_grad, 'enc', axis=0, tiled=True)  7.53 us
    ppermute x2, waiting for transfers between devices, body(): earlier.append(lax.ppermute(earlier[-1], ('enc', 'rep'), up))  6.27 us
    select_n x4, other arithmetic, tile(): piece_coef = jnp.where(piece_offsets < anchor_count, piece_coef, 0.0)  5.74 us
    unnamed x14, local copies, waits for them, and re-layouts  3.77 us
  transfers between devices with their start and end apart: 9, of which 9 were waited for; matrix products, arithmetic and copies ran while one was open for 6% of the time, Pallas kernels for 0%

profile of v1, /device:TPU:0, one launch (start us, length us, event | category | flops | bytes accessed | tf_op | source)
XLA Modules:
  0.0 175.4 jit_solution(8248045239394809225)
XLA Ops:
  7.2 1.0 copy-done
  8.2 2.2 %fusion.40 = f32[256,768]{1,0:T(8,128)} fusion(bf16[256,384]{1,0:T(8,128)(2,1)} %param.6, bf16[384,768]{1,0:T(8,128)(2,1)S(1)} %copy-done), kind=kOutput, calls=%fused_computation.65 | convolution fusion | flops 150994944 | bytes 1572864 | tf_op jit(solution)/shard_map/dot_general | solution.py:31
  10.5 0.6 dynamic_slice.41
  11.1 0.8 dynamic_slice.43
  11.9 19.2 %reduce-scatter.3.cloned.1.call-done = f32[128,768]{1,0:T(8,128)} async-done(((f32[256,768]{1,0:T(8,128)}), f32[128,768]{1,0:T(8,128)}) %reduce-scatter.3.cloned.1.call-update) | async-done | bytes 393232 | tf_op jit(solution)/shard_map/reduce_scatter | solution.py:30
  31.0 1.1 multiply_reduce_fusion.1
  32.3 5.0 %collective-permute-done.1 = bf16[128,768]{1,0:T(8,128)(2,1)S(1)} collective-permute-done((bf16[128,768]{1,0:T(8,128)(2,1)S(1)}, bf16[128,768]{1,0:T(8,128)(2,1)S(1)}, u32[]{:S(2)}, u32[]{:S(2)}) %collective-permute-start.1) | collective-permute-done | bytes 196640 | tf_op jit(solution)/shard_map/ppermute | solution.py:41
  37.3 0.7 compare_select_fusion.1
  38.0 1.4 compare_select_fusion.2
  39.4 1.7 collective-permute-start.3
  41.1 1.3 collective-permute-done.2
  42.4 1.9 %collective-permute-done.3 = bf16[128,768]{1,0:T(8,128)(2,1)S(1)} collective-permute-done((bf16[128,768]{1,0:T(8,128)(2,1)S(1)}, bf16[128,768]{1,0:T(8,128)(2,1)S(1)}, u32[]{:S(2)}, u32[]{:S(2)}) %collective-permute-start.3) | collective-permute-done | bytes 196640 | tf_op jit(solution)/shard_map/ppermute | solution.py:43
  45.6 29.0 %while.23 = (s32[]{:T(128)}, bf16[128,768]{1,0:T(8,128)(2,1)S(1)}, f32[512,768]{1,0:T(8,128)S(1)}, f32[512]{0:T(512)S(1)}, s32[]{:T(128)}, /*index=5*/s32[4]{0:T...) while((s32[]{:T(128)}, bf16[128,768]{1,0:T(8,128)(2,1)S(1)}, ...), condition=%wide.region_7.8_spmd.clone.clone, body=%wide.region_4.7_spmd.clone.clone.sunk | while | flops 203260192 | bytes 6246334 | solution.py:98
  45.6 1.5 collective-permute-start
  47.1 0.7 dynamic_slice.56
  47.8 1.5 compare_select_fusion.4
  49.3 5.6 %collective-permute-done = bf16[128,768]{1,0:T(8,128)(2,1)S(1)} collective-permute-done((bf16[128,768]{1,0:T(8,128)(2,1)S(1)}, bf16[128,768]{1,0:T(8,128)(2,1)S(1)}, u32[]{:S(2)}, u32[]{:S(2)}) %collective-permute-start) | collective-permute-done | bytes 196640 | tf_op jit(solution)/shard_map/while/body/eval_jaxpr/ppermute | solution.py:12
  56.2 0.7 dynamic_slice.56
  56.8 1.5 compare_select_fusion.4
  58.3 6.3 %collective-permute-done = bf16[128,768]{1,0:T(8,128)(2,1)S(1)} collective-permute-done((bf16[128,768]{1,0:T(8,128)(2,1)S(1)}, bf16[128,768]{1,0:T(8,128)(2,1)S(1)}, u32[]{:S(2)}, u32[]{:S(2)}) %collective-permute-start) | collective-permute-done | bytes 196640 | tf_op jit(solution)/shard_map/while/body/eval_jaxpr/ppermute | solution.py:12
  65.2 0.6 convolution_add_fusion.2
  65.9 0.7 dynamic_slice.56
  66.5 1.5 compare_select_fusion.4
  68.0 5.4 %collective-permute-done = bf16[128,768]{1,0:T(8,128)(2,1)S(1)} collective-permute-done((bf16[128,768]{1,0:T(8,128)(2,1)S(1)}, bf16[128,768]{1,0:T(8,128)(2,1)S(1)}, u32[]{:S(2)}, u32[]{:S(2)}) %collective-permute-start) | collective-permute-done | bytes 196640 | tf_op jit(solution)/shard_map/while/body/eval_jaxpr/ppermute | solution.py:12
  74.0 0.6 convolution_add_fusion.2
  74.6 1.1 fusion.21
  75.8 21.7 %reduce-scatter.5.cloned.1.call-done = bf16[128,768]{1,0:T(8,128)(2,1)} async-done(((bf16[512,768]{1,0:T(8,128)(2,1)}), bf16[128,768]{1,0:T(8,128)(2,1)}) %reduce-scatter.5.cloned.1.call-update) | async-done | bytes 196624 | tf_op jit(solution)/shard_map/reduce_scatter | solution.py:101
  97.5 7.5 %all_gather.3 = bf16[256,768]{1,0:T(8,128)(2,1)S(1)} all-gather(bf16[128,768]{1,0:T(8,128)(2,1)} %reduce-scatter.5.cloned.1.call-done), channel_id=1, replica_groups=mesh['groups'=2,'loop'=4,'enc'=2,'rep'=2] {'enc'}, dimensions={0}, use_global_device_ids=true | all-gather | bytes 589824 | tf_op jit(solution)/shard_map/all_gather | solution.py:104
  105.1 1.4 convolution_bitcast_fusion
  106.5 1.1 convolution_convert_fusion
  107.6 58.7 %all-reduce.2.cloned.1.call-done = f32[384,768]{0,1:T(8,128)} async-done(((f32[384,768]{0,1:T(8,128)}), f32[384,768]{0,1:T(8,128)}) %all-reduce.2.cloned.1.call-update) | async-done | bytes 1179664 | tf_op jit(solution)/shard_map/psum | solution.py:114
  166.2 2.7 %copy.9 = f32[384,768]{1,0:T(8,128)} copy(f32[384,768]{0,1:T(8,128)} %all-reduce.2.cloned.1.call-done) | data formatting | bytes 2359296
  (42 shorter events, 4.1 us)
Async XLA Ops:
  7.2 1.1 copy-start
  7.2 3.3 %copy-start.2 = (s32[4]{0:T(128)S(1)}, s32[4]{0:T(128)}, u32[]{:S(2)}) copy-start(s32[4]{0:T(128)} %param.9) | copy-start | bytes 52
  7.2 23.8 %reduce-scatter.3.cloned.1.call-start = ((), (), s32[]{:S(2)}) async-start(), calls=%async_computation.2 | async-start | bytes 1179648 | tf_op jit(solution)/shard_map/reduce_scatter | solution.py:30
  10.4 87.1 %reduce-scatter.5.cloned.1.call-start = ((), (), s32[]{:S(2)}) async-start(), calls=%async_computation.3 | async-start | bytes 983040 | tf_op jit(solution)/shard_map/reduce_scatter | solution.py:101
  32.1 5.1 %collective-permute-start.1 = (bf16[128,768]{1,0:T(8,128)(2,1)S(1)}, bf16[128,768]{1,0:T(8,128)(2,1)S(1)}, u32[]{:S(2)}, u32[]{:S(2)}) collective-permute-start(bf16[128,768]{1,0:T(8,128)(2,1)S(1)} %get-tuple-element.543), channel_id=1, source_target_pairs={{0,1},{1,2},{2,3},{3,0},{4,5},{5,6},{6,7},{7,4},{8,9},{9,10},{10,1... | collective-permute-start | bytes 589832 | tf_op jit(solution)/shard_map/ppermute | solution.py:41
  37.3 5.1 %collective-permute-start.2 = (bf16[128,768]{1,0:T(8,128)(2,1)S(1)}, bf16[128,768]{1,0:T(8,128)(2,1)S(1)}, u32[]{:S(2)}, u32[]{:S(2)}) collective-permute-start(bf16[128,768]{1,0:T(8,128)(2,1)S(1)} %collective-permute-done.1), channel_id=1, source_target_pairs={{0,1},{1,2},{2,3},{3,0},{4,5},{5,6},{6,7},{7,4},{8,9},{9,10},{10,1... | collective-permute-start | bytes 589832 | tf_op jit(solution)/shard_map/ppermute | solution.py:41
  39.4 4.9 %collective-permute-start.3 = (bf16[128,768]{1,0:T(8,128)(2,1)S(1)}, bf16[128,768]{1,0:T(8,128)(2,1)S(1)}, u32[]{:S(2)}, u32[]{:S(2)}) collective-permute-start(bf16[128,768]{1,0:T(8,128)(2,1)S(1)} %get-tuple-element.543), channel_id=1, source_target_pairs={{0,3},{1,0},{2,1},{3,2},{4,7},{5,4},{6,5},{7,6},{8,11},{9,8},{10,9... | collective-permute-start | bytes 589832 | tf_op jit(solution)/shard_map/ppermute | solution.py:43
  45.6 9.3 %collective-permute-start = (bf16[128,768]{1,0:T(8,128)(2,1)S(1)}, bf16[128,768]{1,0:T(8,128)(2,1)S(1)}, u32[]{:S(2)}, u32[]{:S(2)}) collective-permute-start(bf16[128,768]{1,0:T(8,128)(2,1)S(1)} %get-tuple-element.560), channel_id=1, source_target_pairs={{0,4},{4,8},{8,12},{12,0},{1,5},{5,9},{9,13},{13,1},{2,6},{6,10},{... | collective-permute-start | bytes 589832 | tf_op jit(solution)/shard_map/while/body/eval_jaxpr/ppermute | solution.py:12
  56.1 8.5 %collective-permute-start = (bf16[128,768]{1,0:T(8,128)(2,1)S(1)}, bf16[128,768]{1,0:T(8,128)(2,1)S(1)}, u32[]{:S(2)}, u32[]{:S(2)}) collective-permute-start(bf16[128,768]{1,0:T(8,128)(2,1)S(1)} %get-tuple-element.560), channel_id=1, source_target_pairs={{0,4},{4,8},{8,12},{12,0},{1,5},{5,9},{9,13},{13,1},{2,6},{6,10},{... | collective-permute-start | bytes 589832 | tf_op jit(solution)/shard_map/while/body/eval_jaxpr/ppermute | solution.py:12
  65.8 7.6 %collective-permute-start = (bf16[128,768]{1,0:T(8,128)(2,1)S(1)}, bf16[128,768]{1,0:T(8,128)(2,1)S(1)}, u32[]{:S(2)}, u32[]{:S(2)}) collective-permute-start(bf16[128,768]{1,0:T(8,128)(2,1)S(1)} %get-tuple-element.560), channel_id=1, source_target_pairs={{0,4},{4,8},{8,12},{12,0},{1,5},{5,9},{9,13},{13,1},{2,6},{6,10},{... | collective-permute-start | bytes 589832 | tf_op jit(solution)/shard_map/while/body/eval_jaxpr/ppermute | solution.py:12
  74.6 30.5 %copy-start.1 = (bf16[256,384]{1,0:T(8,128)(2,1)S(1)}, bf16[256,384]{1,0:T(8,128)(2,1)}, u32[]{:S(2)}) copy-start(bf16[256,384]{1,0:T(8,128)(2,1)} %param.6) | copy-start | bytes 589828
  75.8 90.5 %all-reduce.2.cloned.1.call-start = ((), (), s32[]{:S(2)}) async-start(), calls=%async_computation.4 | async-start | bytes 2359296 | tf_op jit(solution)/shard_map/psum | solution.py:114
Sparse Core Ops, SparseCore 0:
  10.8 20.1 reduce-scatter.2
  75.9 21.6 reduce-scatter.4
  106.6 59.5 all-reduce.1
